TPU v7x, 128 devices: a whole 4x4x4 slice. The times are simulated.
128 devices in a mesh: lat: 4 (over z), lon: 32 (over x, y, core).
Axes of the slice: x: 4, y: 4, z: 4, core: 2. Of those that a mesh axis runs over, the one named last changes fastest.
Arguments:
- obs_tiles: bfloat16 [128, 128, 4, 8, 256], P(('lat', 'lon'))
- tile_block: int32 [128, 128, 4], P(('lat', 'lon')), may hold values from 0 to 11
- tile_rows: int32 [128, 128, 4], P(('lat', 'lon')), may hold values from 0 to 256, as said below
- embed_weight: bfloat16 [6, 23], replicated, may hold values from -2.5 to 2.5
- conv1_weight: bfloat16 [9, 24, 256], replicated, may hold values from -0.4375 to 0.4375
- conv1_bias: float32 [256], replicated, may hold values from -3 to 3
- conv2_weight: bfloat16 [9, 256, 512], replicated, may hold values from -0.125 to 0.125
- conv2_bias: float32 [512], replicated, may hold values from -3 to 3
Outputs:
- coarse: bfloat16 [64, 384, 512], P('lat')
Inputs may be any that keep to these rules, and one draw needn't show every extreme that they name: `tile_rows`: for each source and destination the live slots come first: all hold 256 rows but the last live one, which holds 1 to 256; later slots hold 0. In every draw one destination block receives 4 live tiles from every source.
All inputs are finite; a program needn't handle non-finite values.
Results may differ from a plain program's by a relative error of at most 0.0052.
Values may be sent and summed in bfloat16 or wider, within the bound.
No kernel may reach another device: no remote copies, remote signals or barrier semaphores. Data moves between devices by JAX's collectives and lax.ppermute only.
A program may use at most 64 MiB of HBM per device.

v0:
```python
import jax
import jax.numpy as jnp
from jax import lax
from jax.sharding import PartitionSpec as P

BX = 64
BY = 48
SB = 16
kernel_scale = 0.5


def shifted(value, axis, by):
    length = lax.axis_size(axis)
    return lax.ppermute(value, axis, [(i, (i + by) % length) for i in range(length)])


def from_behind(block, axis, distance):
    devices = range(lax.axis_size(axis))
    route = [(i - distance, i) for i in devices if i - distance in devices]
    return lax.ppermute(block, axis, route)


def tile_terms(tiles, row_count, embed_weight):
    cell_ids = jnp.arange(SB * SB, dtype=jnp.int32)
    center_row = (cell_ids // SB).astype(jnp.float32) + 0.5
    center_col = (cell_ids % SB).astype(jnp.float32) + 0.5
    place_row = tiles[:, 0, :].astype(jnp.float32)
    place_col = tiles[:, 1, :].astype(jnp.float32)
    distance = (center_row[None, :, None] - place_row[:, None, :]) ** 2 + (
        center_col[None, :, None] - place_col[:, None, :]
    ) ** 2
    is_live = jnp.arange(tiles.shape[2], dtype=jnp.int32)[None, None, :] < row_count[:, None, None]
    kernel = jnp.where(is_live, jnp.exp(-distance * kernel_scale), jnp.float32(0.0)).astype(
        jnp.bfloat16
    )
    embedded = jnp.einsum(
        "tvo,vc->tco", tiles[:, 2:, :], embed_weight, preferred_element_type=jnp.float32
    ).astype(jnp.bfloat16)
    features = jnp.concatenate(
        [jnp.ones((tiles.shape[0], 1, tiles.shape[2]), jnp.bfloat16), embedded], axis=1
    )
    return jnp.einsum("tco,tko->tck", features, kernel, preferred_element_type=jnp.float32)


def stride_conv(padded, weight, out_rows, out_cols):
    running = jnp.zeros((out_rows * out_cols, weight.shape[2]), jnp.float32)
    for row_tap in range(3):
        for col_tap in range(3):
            tap_rows = lax.slice(
                padded,
                (row_tap, col_tap, 0),
                (row_tap + 2 * out_rows - 1, col_tap + 2 * out_cols - 1, padded.shape[2]),
                (2, 2, 1),
            )
            running = running + jnp.dot(
                tap_rows.reshape(-1, padded.shape[2]),
                weight[3 * row_tap + col_tap],
                preferred_element_type=jnp.float32,
            )
    return running.reshape(out_rows, out_cols, weight.shape[2])


def shards(
    obs_tiles,
    tile_block,
    tile_rows,
    embed_weight,
    conv1_weight,
    conv1_bias,
    conv2_weight,
    conv2_bias,
):
    block_count = obs_tiles.shape[1]
    slot_count = obs_tiles.shape[2]
    feat_rows = obs_tiles.shape[3]
    tile_len = obs_tiles.shape[4]
    arrived_all = (
        lax.all_to_all(obs_tiles, ("lat", "lon"), split_axis=1, concat_axis=0, tiled=True),
        lax.all_to_all(tile_block, ("lat", "lon"), split_axis=1, concat_axis=0, tiled=True),
        lax.all_to_all(tile_rows, ("lat", "lon"), split_axis=1, concat_axis=0, tiled=True),
    )
    group_count = block_count // 8
    group_size = 8 * slot_count
    arrived = arrived_all[0].reshape(group_count, group_size, feat_rows, tile_len)
    block_ids = arrived_all[1].reshape(group_count, group_size)
    row_count = arrived_all[2].reshape(group_count, group_size)
    sub_count = BX // SB * (BY // SB)
    channel_count = conv1_weight.shape[1]

    def add_group(running, inputs):
        tiles, group_ids, group_rows = inputs
        tile_sums = tile_terms(tiles, group_rows, embed_weight)
        onehot = (group_ids[:, None] == jnp.arange(sub_count, dtype=jnp.int32)[None, :]).astype(
            jnp.float32
        )
        return (
            running + jnp.einsum("ts,tck->sck", onehot, tile_sums, precision=lax.Precision.HIGHEST),
            None,
        )

    start = jnp.zeros((sub_count, channel_count, tile_len), jnp.float32)
    block_sums, _ = lax.scan(add_group, start, (arrived, block_ids, row_count))
    density = block_sums[:, 0, :]
    data_part = block_sums[:, 1:, :] / (1.0 + density[:, None, :])
    channels = jnp.concatenate([jnp.log1p(density)[:, None, :], data_part], axis=1).astype(
        jnp.bfloat16
    )
    grid_field = (
        channels.reshape(BX // SB, BY // SB, channel_count, SB, SB)
        .transpose(0, 3, 1, 4, 2)
        .reshape(BX, BY, channel_count)
    )
    rim_width = 1
    side_rim = shifted(grid_field[:, BY - rim_width :, :], "lon", 1)
    padded = jnp.concatenate([side_rim, grid_field], axis=1)
    top_rim = from_behind(padded[BX - rim_width :, :, :], "lat", 1)
    padded = jnp.concatenate([top_rim, padded], axis=0)
    first_layer = jax.nn.silu(
        stride_conv(padded, conv1_weight, BX // 2, BY // 2) + conv1_bias
    ).astype(jnp.bfloat16)
    first_side = shifted(first_layer[:, BY // 2 - 1 :, :], "lon", 1)
    first_padded = jnp.concatenate([first_side, first_layer], axis=1)
    first_top = from_behind(first_padded[BX // 2 - 1 :, :, :], "lat", 1)
    first_padded = jnp.concatenate([first_top, first_padded], axis=0)
    coarse = (stride_conv(first_padded, conv2_weight, BX // 4, BY // 4) + conv2_bias).astype(
        jnp.bfloat16
    )
    return lax.all_gather(coarse, "lon", axis=1, tiled=True)


def solution(mesh):
    placed = (
        P(("lat", "lon"), None, None, None, None),
        P(("lat", "lon"), None, None),
        P(("lat", "lon"), None, None),
        P(),
        P(),
        P(),
        P(),
        P(),
    )
    return jax.shard_map(
        shards, mesh=mesh, in_specs=placed, out_specs=P("lat", None, None), check_vma=False
    )
```

profile of v0, /device:TPU:1, one launch (start us, length us, event | category | flops | bytes accessed | tf_op | source)
XLA Modules:
  0.0 268.7 jit_solution(6266015869091623327)
XLA Ops:
  6.5 1.4 copy.26
  8.0 11.5 %all-to-all-start = ((s32[1,128,4]{2,0,1:T(1,128)}), s32[1,128,4]{2,0,1:T(1,128)S(1)}, u32[]{:S(2)}, u32[]{:S(2)}) async-start(s32[1,128,4]{2,0,1:T(1,128)} %copy.26), calls=%async_computation | async-start | bytes 131072 | tf_op jit(solution)/shard_map/all_to_all | solution.py:79
  19.5 0.8 copy.28
  20.3 8.7 %all-to-all-done = s32[1,128,4]{2,0,1:T(1,128)S(1)} async-done(((s32[1,128,4]{2,0,1:T(1,128)}), s32[1,128,4]{2,0,1:T(1,128)S(1)}, u32[]{:S(2)}, u32[]{:S(2)}) %all-to-all-start) | async-done | bytes 2080 | tf_op jit(solution)/shard_map/all_to_all | solution.py:79
  29.0 13.8 %all_to_all.12 = s32[1,128,4]{2,0,1:T(1,128)S(1)} all-to-all(s32[1,128,4]{2,0,1:T(1,128)S(1)} %copy.28), channel_id=1, replica_groups=mesh['lat'=4,'lon'=32] {'lat','lon'}, dimensions={1} | all-to-all | bytes 4096 | tf_op jit(solution)/shard_map/all_to_all | solution.py:80
  42.8 4.4 %all-to-all-start.1 = ((bf16[1,128,4,8,256]{4,3,2,0,1:T(8,128)(2,1)}), bf16[1,128,4,8,256]{4,3,2,0,1:T(8,128)(2,1)S(1)}, u32[]{:S(2)}, u32[]{:S(2)}) async-start(bf16[1,128,4,8,256]{4,3,2,0,1:T(8,128)(2,1)} %bitcast.136), calls=%async_computation.1 | async-start | bytes 4194304 | tf_op jit(solution)/shard_map/all_to_all | solution.py:78
  47.8 0.8 reduce.6
  48.6 0.8 reduce.7
  49.5 28.2 %all-to-all-done.1 = bf16[1,128,4,8,256]{4,3,2,0,1:T(8,128)(2,1)S(1)} async-done(((bf16[1,128,4,8,256]{4,3,2,0,1:T(8,128)(2,1)}), bf16[1,128,4,8,256]{4,3,2,0,1:T(8,128)(2,1)S(1)}, u32[]{:S(2)}, u32[]{:S(2)}) %all-to-all-start.1) | async-done | bytes 2097184 | tf_op jit(solution)/shard_map/all_to_all | solution.py:78
  77.7 61.0 %while.13 = (s32[]{:T(128)}, f32[12,24,256]{2,0,1:T(8,128)S(1)}, s32[16,32]{1,0:T(8,128)S(1)}, bf16[16,32,8,256]{3,2,1,0:T(8,128)(2,1)S(1)}, bf16[6,23]{1,0:T(8,...) while((s32[]{:T(128)}, f32[12,24,256]{2,0,1:T(8,128)S(1)}, ...), condition=%wide.region_1.2_spmd.clone, body=%wide.region_0.1_spmd.clone.sunk | while | flops 150475136 | bytes 3626115 | solution.py:102
  78.2 2.7 fusion.104
  82.0 2.7 fusion.104
  85.8 2.7 fusion.104
  89.6 2.7 fusion.104
  93.5 2.7 fusion.104
  97.3 2.7 fusion.104
  101.1 2.7 fusion.104
  104.9 2.7 fusion.104
  108.7 2.7 fusion.104
  112.5 2.7 fusion.104
  116.3 2.7 fusion.104
  120.2 2.7 fusion.104
  124.0 2.7 fusion.104
  127.8 2.7 fusion.104
  131.6 2.7 fusion.104
  135.4 2.7 fusion.104
  139.0 0.8 concatenate.25
  140.0 1.1 copy.30
  141.8 1.6 slice.164
  143.4 1.7 slice.162
  145.1 0.8 slice.158
  145.9 0.8 slice.156
  146.8 0.8 collective-permute-start
  147.6 0.9 fusion.53
  148.6 1.8 fusion.51
  150.4 0.9 fusion.48
  151.3 0.9 fusion.46
  152.9 0.8 copy.31
  153.8 0.9 fusion.25
  154.7 2.0 collective-permute-start.1
  156.7 3.7 %slice.160 = bf16[32,24,24]{0,2,1:T(8,128)(2,1)S(1)} slice(bf16[64,49,24]{0,2,1:T(8,128)(2,1)S(1)} %pad_maximum_fusion.1), slice={[1:64:2], [0:47:2], [0:24:1]} | slice | bytes 73728 | tf_op jit(solution)/shard_map/slice | solution.py:49
  160.4 3.7 %slice.154 = bf16[32,24,24]{0,2,1:T(8,128)(2,1)S(1)} slice(bf16[64,49,24]{0,2,1:T(8,128)(2,1)S(1)} %pad_maximum_fusion.1), slice={[0:63:2], [0:47:2], [0:24:1]} | slice | bytes 73728 | tf_op jit(solution)/shard_map/slice | solution.py:49
  164.3 0.9 reshape.154
  165.3 0.9 reshape.157
  166.2 1.1 maximum_maximum_fusion.1
  167.3 4.2 %slice.152 = bf16[32,24,24]{0,2,1:T(8,128)(2,1)S(1)} slice(bf16[65,49,24]{0,2,1:T(8,128)(2,1)S(1)} %maximum_maximum_fusion.1), slice={[0:63:2], [2:49:2], [0:24:1]} | slice | bytes 73728 | tf_op jit(solution)/shard_map/slice | solution.py:49
  171.5 3.7 %slice.150 = bf16[32,24,24]{0,2,1:T(8,128)(2,1)S(1)} slice(bf16[65,49,24]{0,2,1:T(8,128)(2,1)S(1)} %maximum_maximum_fusion.1), slice={[0:63:2], [1:48:2], [0:24:1]} | slice | bytes 73728 | tf_op jit(solution)/shard_map/slice | solution.py:49
  175.2 3.7 %slice.148 = bf16[32,24,24]{0,2,1:T(8,128)(2,1)S(1)} slice(bf16[65,49,24]{0,2,1:T(8,128)(2,1)S(1)} %maximum_maximum_fusion.1), slice={[0:63:2], [0:47:2], [0:24:1]} | slice | bytes 73728 | tf_op jit(solution)/shard_map/slice | solution.py:49
  179.4 0.9 reshape.151
  180.8 1.1 fusion.58
  181.8 1.0 convolution_add_fusion.4
  182.8 1.0 convolution_add_fusion.3
  183.9 1.0 fusion.23
  184.9 1.0 fusion.24
  186.3 0.7 slice.184
  187.0 0.8 slice.182
  188.6 0.7 reshape.169
  189.3 0.7 reshape.168
  191.9 2.1 collective-permute-start.3
  194.2 0.7 slice.180
  196.0 1.0 maximum_maximum_fusion
  200.5 0.8 copy.38
  201.4 51.4 %all-gather.2.cloned.1.call-done = bf16[16,384,512]{2,0,1:T(8,128)(2,1)} async-done(((bf16[16,12,512]{2,0,1:T(8,128)(2,1)}), bf16[16,384,512]{2,0,1:T(8,128)(2,1)}) %all-gather.2.cloned.1.call-update) | async-done | bytes 6291472 | tf_op jit(solution)/shard_map/all_gather | solution.py:128
  252.8 9.0 %copy.39 = bf16[16,384,512]{2,1,0:T(8,128)(2,1)} copy(bf16[16,384,512]{2,0,1:T(8,128)(2,1)} %all-gather.2.cloned.1.call-done) | data formatting | bytes 12582912 | tf_op jit(solution)/shard_map/all_gather | solution.py:128
  (208 shorter events, 29.1 us)
Async XLA Ops:
  8.0 21.0 %all-to-all-start = ((s32[1,128,4]{2,0,1:T(1,128)}), s32[1,128,4]{2,0,1:T(1,128)S(1)}, u32[]{:S(2)}, u32[]{:S(2)}) async-start(s32[1,128,4]{2,0,1:T(1,128)} %copy.26), calls=%async_computation | async-start | bytes 131072 | tf_op jit(solution)/shard_map/all_to_all | solution.py:79
  20.2 57.5 %copy-start.10 = (bf16[6,23]{1,0:T(8,128)(2,1)S(1)}, bf16[6,23]{1,0:T(8,128)(2,1)}, u32[]{:S(2)}) copy-start(bf16[6,23]{1,0:T(8,128)(2,1)} %param.13) | copy-start | bytes 832
  42.8 34.9 %all-to-all-start.1 = ((bf16[1,128,4,8,256]{4,3,2,0,1:T(8,128)(2,1)}), bf16[1,128,4,8,256]{4,3,2,0,1:T(8,128)(2,1)S(1)}, u32[]{:S(2)}, u32[]{:S(2)}) async-start(bf16[1,128,4,8,256]{4,3,2,0,1:T(8,128)(2,1)} %bitcast.136), calls=%async_computation.1 | async-start | bytes 4194304 | tf_op jit(solution)/shard_map/all_to_all | solution.py:78
  47.2 205.6 %all-gather.2.cloned.1.call-start = ((), (), s32[]{:S(2)}) async-start(), calls=%async_computation.3 | async-start | bytes 6488064 | tf_op jit(solution)/shard_map/all_gather | solution.py:128
  146.8 6.2 %collective-permute-start = (bf16[64,1,24]{2,1,0:T(2,128)(2,1)}, bf16[64,1,24]{2,1,0:T(2,128)(2,1)}, u32[]{:S(2)}, u32[]{:S(2)}) collective-permute-start(bf16[64,1,24]{2,1,0:T(2,128)(2,1)} %slice.192), channel_id=1, source_target_pairs={{0,1},{1,2},{2,3},{3,4},{4,5},{5,6},{6,7},{7,8},{8,9},{9,10},{10,1... | collective-permute-start | bytes 9224 | tf_op jit(solution)/shard_map/ppermute | solution.py:14
  154.7 11.5 %collective-permute-start.1 = (bf16[1,49,24]{0,2,1:T(8,128)(2,1)}, bf16[1,49,24]{0,2,1:T(8,128)(2,1)}, u32[]{:S(2)}, u32[]{:S(2)}) collective-permute-start(bf16[1,49,24]{0,2,1:T(8,128)(2,1)} %fusion.25), channel_id=1, source_target_pairs={{0,32},{32,64},{64,96},{1,33},{33,65},{65,97},{2,34},{34,66},{66,9... | collective-permute-start | bytes 7064 | tf_op jit(solution)/shard_map/ppermute | solution.py:20
  180.3 3.5 %copy-start = (f32[768,256]{1,0:T(8,128)S(1)}, f32[768,256]{1,0:T(8,128)}, u32[]{:S(2)}) copy-start(f32[768,256]{1,0:T(8,128)} %fusion.51) | copy-start | bytes 2359300
  180.5 3.4 %copy-start.9 = (bf16[768,24]{0,1:T(8,128)(2,1)S(1)}, bf16[768,24]{0,1:T(8,128)(2,1)}, u32[]{:S(2)}) copy-start(bf16[768,24]{0,1:T(8,128)(2,1)} %reshape.154) | copy-start | bytes 110596
  182.8 2.1 copy-start.8
  184.9 1.0 copy-start.12
  186.2 5.1 %collective-permute-start.2 = (bf16[32,1,256]{2,1,0:T(2,128)(2,1)S(1)}, bf16[32,1,256]{2,1,0:T(2,128)(2,1)S(1)}, u32[]{:S(2)}, u32[]{:S(2)}) collective-permute-start(bf16[32,1,256]{2,1,0:T(2,128)(2,1)S(1)} %slice.195), channel_id=1, source_target_pairs={{0,1},{1,2},{2,3},{3,4},{4,5},{5,6},{6,7},{7,8},{8,9},{9,10},{10,1... | collective-permute-start | bytes 49160 | tf_op jit(solution)/shard_map/ppermute | solution.py:14
  191.3 7.1 %copy-start.1 = (bf16[9,256,512]{2,1,0:T(8,128)(2,1)S(1)}, bf16[9,256,512]{2,1,0:T(8,128)(2,1)}, u32[]{:S(2)}) copy-start(bf16[9,256,512]{2,1,0:T(8,128)(2,1)} %param.16) | copy-start | bytes 7077892
  191.3 2.7 copy-start.7
  191.9 4.1 %collective-permute-start.3 = (bf16[1,25,256]{2,1,0:T(8,128)(2,1)}, bf16[1,25,256]{2,1,0:T(8,128)(2,1)S(1)}, u32[]{:S(2)}, u32[]{:S(2)}) collective-permute-start(bf16[1,25,256]{2,1,0:T(8,128)(2,1)} %fusion.45), channel_id=1, source_target_pairs={{0,32},{32,64},{64,96},{1,33},{33,65},{65,97},{2,34},{34,66},{66,9... | collective-permute-start | bytes 38408 | tf_op jit(solution)/shard_map/ppermute | solution.py:20
  197.0 2.0 copy-start.6
  198.3 1.0 copy-start.5
  198.6 0.9 copy-start.4
  199.1 0.9 copy-start.3
  199.3 0.9 copy-start.2
  199.7 0.7 copy-start.11
Sparse Core Ops, SparseCore 0:
  201.5 51.2 all-gather.1
where the time goes:
time: 270 us; the launch traced here: 269 us
  waiting for transfers between devices  88.4 us (33%)
  matrix products  69.2 us (26%)
  local copies, waits for them, and re-layouts  53.3 us (20%)
  starting transfers between devices  20.9 us (8%)
  between operations  14 us (5%)
  blocking collectives  13.8 us (5%)
  other arithmetic  7.95 us (3%)
    all_gather x1, waiting for transfers between devices, shards(): return lax.all_gather(coarse, 'lon', axis=1, tiled=True)  51.4 us
    dot_general x16, matrix products, tile_terms(): jnp.einsum('tco,tko->tck', features, kernel, preferred_element_type=jnp.f...  42.6 us
    slice x23, local copies, waits for them, and re-layouts, stride_conv(): lax.slice(padded, (row_tap, col_tap, 0), (row_tap + 2 * out_rows - 1, col...  29.3 us
    all_to_all x1, waiting for transfers between devices, shards(): lax.all_to_all(obs_tiles, ('lat', 'lon'), split_axis=1, concat_axis=0, ti...  28.2 us
    all_to_all x1, blocking collectives, shards(): lax.all_to_all(tile_rows, ('lat', 'lon'), split_axis=1, concat_axis=0, ti...  13.8 us
    dot_general x18, matrix products, stride_conv(): jnp.dot(tap_rows.reshape(-1, padded.shape[2]), weight[3 * row_tap + col_t...  11.6 us
    all_to_all x1, starting transfers between devices, shards(): lax.all_to_all(tile_block, ('lat', 'lon'), split_axis=1, concat_axis=0, t...  11.5 us
    dot_general x16, matrix products, add_group(): jnp.einsum('ts,tck->sck', onehot, tile_sums, precision=lax.Precision.HIGH...  10.1 us
  transfers between devices with their start and end apart: 7, of which 3 were waited for; matrix products, arithmetic and copies ran while one was open for 9% of the time, Pallas kernels for 0%

commit v1 on v0

--- a/solution.py
+++ b/solution.py
@@ -7,6 +7,12 @@
 BY = 48
 SB = 16
 kernel_scale = 0.5
+
+
+def exchange_blocks(x, mesh_axis, split, join):
+    shards = jnp.split(x, lax.axis_size(mesh_axis), axis=split)
+    incoming = lax.all_to_all(jnp.stack(shards), mesh_axis, 0, 0)
+    return jnp.concatenate(incoming, axis=join)
 
 
 def shifted(value, axis, by):
@@ -77,7 +83,7 @@
     arrived_all = (
         lax.all_to_all(obs_tiles, ("lat", "lon"), split_axis=1, concat_axis=0, tiled=True),
         lax.all_to_all(tile_block, ("lat", "lon"), split_axis=1, concat_axis=0, tiled=True),
-        lax.all_to_all(tile_rows, ("lat", "lon"), split_axis=1, concat_axis=0, tiled=True),
+        exchange_blocks(tile_rows, ("lat", "lon"), 1, 0),
     )
     group_count = block_count // 8
     group_size = 8 * slot_count

time: 270 us -> 345 us (1.28)
  local copies, waits for them, and re-layouts: 53.3 us -> 129 us
    unnamed x28 -> x154, local copies, waits for them, and re-layouts: 2.3 us -> 65.8 us
    split x0 -> x7, local copies, waits for them, and re-layouts: none -> 13 us  [exchange_blocks(): shards = jnp.split(x, lax.axis_size(mesh_axis), axis=split)]
  transfers between devices with their start and end apart: 7 -> 7, of which waited for: 3 -> 3; matrix products, arithmetic and copies ran while one was open for 9% -> 7% of each run, Pallas kernels for 0% -> 0%
where the time goes in v1:
time: 345 us; the launch traced here: 344 us
  local copies, waits for them, and re-layouts  129 us (37%)
  waiting for transfers between devices  87.9 us (25%)
  matrix products  69.2 us (20%)
  starting transfers between devices  20.9 us (6%)
  between operations  14.1 us (4%)
  blocking collectives  13.8 us (4%)
  other arithmetic  8.09 us (2%)
    unnamed x154, local copies, waits for them, and re-layouts  65.8 us
    all_gather x1, waiting for transfers between devices, shards(): return lax.all_gather(coarse, 'lon', axis=1, tiled=True)  51.1 us
    dot_general x16, matrix products, tile_terms(): jnp.einsum('tco,tko->tck', features, kernel, preferred_element_type=jnp.f...  42.6 us
    slice x23, local copies, waits for them, and re-layouts, stride_conv(): lax.slice(padded, (row_tap, col_tap, 0), (row_tap + 2 * out_rows - 1, col...  29.4 us
    all_to_all x1, waiting for transfers between devices, shards(): lax.all_to_all(obs_tiles, ('lat', 'lon'), split_axis=1, concat_axis=0, ti...  28 us
    all_to_all x1, blocking collectives, shards(): lax.all_to_all(tile_block, ('lat', 'lon'), split_axis=1, concat_axis=0, t...  13.8 us
    split x7, local copies, waits for them, and re-layouts, exchange_blocks(): shards = jnp.split(x, lax.axis_size(mesh_axis), axis=split)  13 us
    dot_general x18, matrix products, stride_conv(): jnp.dot(tap_rows.reshape(-1, padded.shape[2]), weight[3 * row_tap + col_t...  11.6 us
  transfers between devices with their start and end apart: 7, of which 3 were waited for; matrix products, arithmetic and copies ran while one was open for 7% of the time, Pallas kernels for 0%

profile of v1, /device:TPU:1, one launch (start us, length us, event | category | flops | bytes accessed | tf_op | source)
XLA Modules:
  0.0 344.1 jit_solution(15599589830242923165)
XLA Ops:
  6.5 1.6 slice_reduce_fusion.114
  8.1 1.9 slice_reduce_fusion.57
  10.0 1.9 slice_reduce_fusion.76
  11.9 1.9 slice_reduce_fusion.95
  13.8 1.9 slice_reduce_fusion.38
  15.7 1.9 slice_reduce_fusion
  17.6 1.9 slice_reduce_fusion.1
  85.0 11.5 %all-to-all-start.2 = ((s32[128,1,1,4]{3,2,1,0:T(1,128)}), s32[128,1,1,4]{3,2,1,0:T(1,128)S(1)}, u32[]{:S(2)}, u32[]{:S(2)}) async-start(s32[128,1,1,4]{3,2,1,0:T(1,128)} %constant_dynamic-update-slice_fusion), calls=%async_computation.2 | async-start | bytes 131072 | tf_op jit(solution)/shard_map/all_to_all | solution.py:14
  96.5 0.8 copy.438
  97.3 8.7 %all-to-all-done.2 = s32[128,1,1,4]{3,2,1,0:T(1,128)S(1)} async-done(((s32[128,1,1,4]{3,2,1,0:T(1,128)}), s32[128,1,1,4]{3,2,1,0:T(1,128)S(1)}, u32[]{:S(2)}, u32[]{:S(2)}) %all-to-all-start.2) | async-done | bytes 2080 | tf_op jit(solution)/shard_map/all_to_all | solution.py:14
  106.1 13.8 %all_to_all.23 = s32[1,128,4]{2,0,1:T(1,128)S(1)} all-to-all(s32[1,128,4]{2,0,1:T(1,128)S(1)} %copy.438), channel_id=1, replica_groups=mesh['lat'=4,'lon'=32] {'lat','lon'}, dimensions={1} | all-to-all | bytes 4096 | tf_op jit(solution)/shard_map/all_to_all | solution.py:85
  119.9 4.4 %all-to-all-start.1 = ((bf16[1,128,4,8,256]{4,3,2,0,1:T(8,128)(2,1)}), bf16[1,128,4,8,256]{4,3,2,0,1:T(8,128)(2,1)S(1)}, u32[]{:S(2)}, u32[]{:S(2)}) async-start(bf16[1,128,4,8,256]{4,3,2,0,1:T(8,128)(2,1)} %bitcast.391), calls=%async_computation.1 | async-start | bytes 4194304 | tf_op jit(solution)/shard_map/all_to_all | solution.py:84
  124.9 0.8 reduce.263
  125.9 0.9 reduce.262
  126.8 28.0 %all-to-all-done.1 = bf16[1,128,4,8,256]{4,3,2,0,1:T(8,128)(2,1)S(1)} async-done(((bf16[1,128,4,8,256]{4,3,2,0,1:T(8,128)(2,1)}), bf16[1,128,4,8,256]{4,3,2,0,1:T(8,128)(2,1)S(1)}, u32[]{:S(2)}, u32[]{:S(2)}) %all-to-all-start.1) | async-done | bytes 2097184 | tf_op jit(solution)/shard_map/all_to_all | solution.py:84
  154.8 61.0 %while.13 = (s32[]{:T(128)}, f32[12,24,256]{2,0,1:T(8,128)S(1)}, s32[16,32]{1,0:T(8,128)S(1)}, bf16[16,32,8,256]{3,2,1,0:T(8,128)(2,1)S(1)}, bf16[6,23]{1,0:T(8,...) while((s32[]{:T(128)}, f32[12,24,256]{2,0,1:T(8,128)S(1)}, ...), condition=%wide.region_1.2_spmd.clone, body=%wide.region_0.1_spmd.clone.sunk | while | flops 150475136 | bytes 3626115 | solution.py:108
  155.3 2.7 fusion.104
  159.1 2.7 fusion.104
  162.9 2.7 fusion.104
  166.7 2.7 fusion.104
  170.5 2.7 fusion.104
  174.4 2.7 fusion.104
  178.2 2.7 fusion.104
  182.0 2.7 fusion.104
  185.8 2.7 fusion.104
  189.6 2.7 fusion.104
  193.4 2.7 fusion.104
  197.2 2.7 fusion.104
  201.1 2.7 fusion.104
  204.9 2.7 fusion.104
  208.7 2.7 fusion.104
  212.5 2.7 fusion.104
  216.0 0.8 concatenate.25
  217.1 1.1 copy.441
  218.2 1.7 slice.164
  219.9 1.7 slice.162
  221.6 0.8 slice.158
  222.4 0.8 slice.156
  223.3 1.0 collective-permute-start
  224.3 0.9 fusion.53
  225.3 1.8 fusion.51
  227.1 0.9 fusion.48
  228.0 0.9 fusion.46
  229.7 0.9 fusion.25
  230.6 2.0 collective-permute-start.1
  232.7 3.7 %slice.160 = bf16[32,24,24]{0,2,1:T(8,128)(2,1)S(1)} slice(bf16[64,49,24]{0,2,1:T(8,128)(2,1)S(1)} %pad_maximum_fusion.1), slice={[1:64:2], [0:47:2], [0:24:1]} | slice | bytes 73728 | tf_op jit(solution)/shard_map/slice | solution.py:55
  236.4 3.7 %slice.154 = bf16[32,24,24]{0,2,1:T(8,128)(2,1)S(1)} slice(bf16[64,49,24]{0,2,1:T(8,128)(2,1)S(1)} %pad_maximum_fusion.1), slice={[0:63:2], [0:47:2], [0:24:1]} | slice | bytes 73728 | tf_op jit(solution)/shard_map/slice | solution.py:55
  240.2 0.9 reshape.146
  241.3 0.9 reshape.149
  242.1 1.1 maximum_maximum_fusion.1
  243.3 4.2 %slice.152 = bf16[32,24,24]{0,2,1:T(8,128)(2,1)S(1)} slice(bf16[65,49,24]{0,2,1:T(8,128)(2,1)S(1)} %maximum_maximum_fusion.1), slice={[0:63:2], [2:49:2], [0:24:1]} | slice | bytes 73728 | tf_op jit(solution)/shard_map/slice | solution.py:55
  247.5 3.7 %slice.150 = bf16[32,24,24]{0,2,1:T(8,128)(2,1)S(1)} slice(bf16[65,49,24]{0,2,1:T(8,128)(2,1)S(1)} %maximum_maximum_fusion.1), slice={[0:63:2], [1:48:2], [0:24:1]} | slice | bytes 73728 | tf_op jit(solution)/shard_map/slice | solution.py:55
  251.1 3.7 %slice.148 = bf16[32,24,24]{0,2,1:T(8,128)(2,1)S(1)} slice(bf16[65,49,24]{0,2,1:T(8,128)(2,1)S(1)} %maximum_maximum_fusion.1), slice={[0:63:2], [0:47:2], [0:24:1]} | slice | bytes 73728 | tf_op jit(solution)/shard_map/slice | solution.py:55
  255.4 0.9 reshape.143
  256.7 1.1 fusion.58
  257.8 1.0 convolution_add_fusion.4
  258.8 1.0 convolution_add_fusion.3
  259.8 1.0 fusion.23
  260.8 1.0 fusion.24
  267.8 1.9 collective-permute-start.3
  271.7 1.0 maximum_maximum_fusion
  276.2 0.8 copy.449
  277.1 51.1 %all-gather.2.cloned.1.call-done = bf16[16,384,512]{2,0,1:T(8,128)(2,1)} async-done(((bf16[16,12,512]{2,0,1:T(8,128)(2,1)}), bf16[16,384,512]{2,0,1:T(8,128)(2,1)}) %all-gather.2.cloned.1.call-update) | async-done | bytes 6291472 | tf_op jit(solution)/shard_map/all_gather | solution.py:134
  328.2 9.0 %copy.450 = bf16[16,384,512]{2,1,0:T(8,128)(2,1)} copy(bf16[16,384,512]{2,0,1:T(8,128)(2,1)} %all-gather.2.cloned.1.call-done) | data formatting | bytes 12582912 | tf_op jit(solution)/shard_map/all_gather | solution.py:134
  (342 shorter events, 97.5 us)
Async XLA Ops:
  85.0 21.0 %all-to-all-start.2 = ((s32[128,1,1,4]{3,2,1,0:T(1,128)}), s32[128,1,1,4]{3,2,1,0:T(1,128)S(1)}, u32[]{:S(2)}, u32[]{:S(2)}) async-start(s32[128,1,1,4]{3,2,1,0:T(1,128)} %constant_dynamic-update-slice_fusion), calls=%async_computation.2 | async-start | bytes 131072 | tf_op jit(solution)/shard_map/all_to_all | solution.py:14
  97.3 57.5 %copy-start.10 = (bf16[6,23]{1,0:T(8,128)(2,1)S(1)}, bf16[6,23]{1,0:T(8,128)(2,1)}, u32[]{:S(2)}) copy-start(bf16[6,23]{1,0:T(8,128)(2,1)} %param.13) | copy-start | bytes 832
  119.9 34.9 %all-to-all-start.1 = ((bf16[1,128,4,8,256]{4,3,2,0,1:T(8,128)(2,1)}), bf16[1,128,4,8,256]{4,3,2,0,1:T(8,128)(2,1)S(1)}, u32[]{:S(2)}, u32[]{:S(2)}) async-start(bf16[1,128,4,8,256]{4,3,2,0,1:T(8,128)(2,1)} %bitcast.391), calls=%async_computation.1 | async-start | bytes 4194304 | tf_op jit(solution)/shard_map/all_to_all | solution.py:84
  124.3 203.9 %all-gather.2.cloned.1.call-start = ((), (), s32[]{:S(2)}) async-start(), calls=%async_computation.3 | async-start | bytes 6488064 | tf_op jit(solution)/shard_map/all_gather | solution.py:134
  223.3 6.4 %collective-permute-start = (bf16[64,1,24]{2,1,0:T(2,128)(2,1)S(1)}, bf16[64,1,24]{2,1,0:T(2,128)(2,1)S(1)}, u32[]{:S(2)}, u32[]{:S(2)}) collective-permute-start(bf16[64,1,24]{2,1,0:T(2,128)(2,1)S(1)} %slice.192), channel_id=1, source_target_pairs={{0,1},{1,2},{2,3},{3,4},{4,5},{5,6},{6,7},{7,8},{8,9},{9,10},{10,1... | collective-permute-start | bytes 9224 | tf_op jit(solution)/shard_map/ppermute | solution.py:20
  230.6 11.5 %collective-permute-start.1 = (bf16[1,49,24]{0,2,1:T(8,128)(2,1)}, bf16[1,49,24]{0,2,1:T(8,128)(2,1)}, u32[]{:S(2)}, u32[]{:S(2)}) collective-permute-start(bf16[1,49,24]{0,2,1:T(8,128)(2,1)} %fusion.25), channel_id=1, source_target_pairs={{0,32},{32,64},{64,96},{1,33},{33,65},{65,97},{2,34},{34,66},{66,9... | collective-permute-start | bytes 7064 | tf_op jit(solution)/shard_map/ppermute | solution.py:26
  256.3 3.5 %copy-start = (f32[768,256]{1,0:T(8,128)S(1)}, f32[768,256]{1,0:T(8,128)}, u32[]{:S(2)}) copy-start(f32[768,256]{1,0:T(8,128)} %fusion.51) | copy-start | bytes 2359300
  256.4 3.4 copy-start.9
  258.8 2.1 copy-start.8
  260.8 1.0 copy-start.12
  262.1 5.1 %collective-permute-start.2 = (bf16[32,1,256]{2,1,0:T(2,128)(2,1)S(1)}, bf16[32,1,256]{2,1,0:T(2,128)(2,1)S(1)}, u32[]{:S(2)}, u32[]{:S(2)}) collective-permute-start(bf16[32,1,256]{2,1,0:T(2,128)(2,1)S(1)} %slice.195), channel_id=1, source_target_pairs={{0,1},{1,2},{2,3},{3,4},{4,5},{5,6},{6,7},{7,8},{8,9},{9,10},{10,1... | collective-permute-start | bytes 49160 | tf_op jit(solution)/shard_map/ppermute | solution.py:20
  267.2 6.9 %copy-start.1 = (bf16[9,256,512]{2,1,0:T(8,128)(2,1)S(1)}, bf16[9,256,512]{2,1,0:T(8,128)(2,1)}, u32[]{:S(2)}) copy-start(bf16[9,256,512]{2,1,0:T(8,128)(2,1)} %param.16) | copy-start | bytes 7077892
  267.2 2.5 copy-start.7
  267.8 3.9 %collective-permute-start.3 = (bf16[1,25,256]{2,1,0:T(8,128)(2,1)}, bf16[1,25,256]{2,1,0:T(8,128)(2,1)S(1)}, u32[]{:S(2)}, u32[]{:S(2)}) collective-permute-start(bf16[1,25,256]{2,1,0:T(8,128)(2,1)} %fusion.45), channel_id=1, source_target_pairs={{0,32},{32,64},{64,96},{1,33},{33,65},{65,97},{2,34},{34,66},{66,9... | collective-permute-start | bytes 38408 | tf_op jit(solution)/shard_map/ppermute | solution.py:26
  272.7 2.0 copy-start.6
  274.0 1.0 copy-start.5
  274.3 0.9 copy-start.4
  274.8 0.9 copy-start.3
  275.0 0.9 copy-start.2
  275.4 0.7 copy-start.11
Sparse Core Ops, SparseCore 0:
  277.2 50.9 all-gather.1
